TPU v7x, 512 devices: a whole 4x8x8 slice. The times are simulated.
512 devices in a mesh: tile: 128 (over z, y, core), grp: 4 (over x).
Axes of the slice: x: 4, y: 8, z: 8, core: 2. Of those that a mesh axis runs over, the one named last changes fastest.
Arguments:
- kelvin_profile: float32 [90, 128, 256], P(None, 'tile'), may hold values from 0.5 to 1.5
- moisture_profile: float32 [90, 128, 256], P(None, 'tile'), may hold values from 0.1 to 3
- spreading_number: float32 [128, 256], P('tile'), may hold values from 0.05 to 0.24
- overhead_angle_measure: float32 [128, 256], P('tile'), may hold values from 0.2 to 1
- illuminated_mask: int32 [128, 256], P('tile'), may hold values 0 or 1
- radiating_tiles: int32 [32768, 1], P('tile'), may hold values from 0 to 127; in each aligned block of 256 rows (0 to 255, 256 to 511, ...) at most 4 rows name the same one
- cloudy_member_factors: float32 [224, 65536], P('grp', 'tile'), may hold values from 0.25 to 2
- arid_opacity_table: float32 [224, 90], P('grp'), may hold values from 0.003 to 0.2
- moisture_attenuation: float32 [224], P('grp'), may hold values from 0.003 to 0.05
- blackbody_share: float32 [224], P('grp'), may hold values from 0.3 to 3
- insolation_per_quadrature: float32 [224], P('grp'), may hold values from 0.3 to 3
Outputs:
- heating: float32 [90, 128, 256], P(None, 'tile')
- temp_next: float32 [90, 128, 256], P(None, 'tile')
- vapour_next: float32 [90, 128, 256], P(None, 'tile')
Inputs may be any that keep to these rules, and one draw needn't show every extreme that they name: `radiating_tiles`: among the columns of one tile no owner is named more than 4 times, a bound that some block reaches.
All inputs are finite; a program needn't handle non-finite values. No bound on the sum of `illuminated_mask` on one device may be relied on, other than what follows from the above.
Results may differ from a plain program's by a relative error of at most 0.00025.
Values sent between devices are 32-bit elements; how exact they have to be, the bound alone decides.
A program may use at most 64 MiB of HBM per device.

v0:
```python
import math
import jax
import jax.numpy as jnp
from jax import lax
from jax.sharding import PartitionSpec as P

NG = 224


def with_halo(block, sides, width):
    for axis, dim in sides:
        count = lax.axis_size(axis)
        forward = [(i, i + 1) for i in range(count - 1)]
        backward = [(target, source) for source, target in forward]
        low = lax.ppermute(
            lax.slice_in_dim(block, block.shape[dim] - width, None, axis=dim), axis, forward
        )
        high = lax.ppermute(lax.slice_in_dim(block, 0, width, axis=dim), axis, backward)
        block = jnp.concatenate([low, block, high], axis=dim)
    return block


def evaluate_warming(
    kelvin_profile,
    moisture_profile,
    overhead_angle_value,
    illuminated_marker,
    profile_window,
    arid_multiplier,
    moisture_multiplier,
    radiance_share_table,
    sunshine_multiplier,
):
    gpoints, strata_mesh = arid_multiplier.shape
    bundle = math.gcd(gpoints, 4)
    bundles = gpoints // bundle
    lower_mask = (jnp.arange(strata_mesh)[None, :] < jnp.arange(strata_mesh + 1)[:, None]).astype(
        jnp.float32
    )
    upper_mask = 1.0 - lower_mask

    def layer_pass(pieces):
        dry_part, vapour_part, radiance_share_piece, solar_part, sub_part = pieces
        thickness = (
            dry_part[:, :, None]
            + (vapour_part[:, None] * sub_part)[:, None, :] * moisture_profile[None]
        )
        column_depth = jnp.einsum(
            "lk,gkm->glm", lower_mask, thickness, precision=lax.Precision.HIGHEST
        )
        growth = jnp.exp(column_depth)
        damped = jnp.exp(-column_depth)
        infrared_radiance = radiance_share_piece[:, None, None] * kelvin_profile[None]
        downward = damped * jnp.einsum(
            "lk,gkm->glm",
            lower_mask,
            infrared_radiance * growth[:, :strata_mesh] * jnp.expm1(thickness),
            precision=lax.Precision.HIGHEST,
        )
        floor_term = infrared_radiance[:, strata_mesh - 1] * damped[:, strata_mesh]
        upward = growth * (
            floor_term[:, None, :]
            - jnp.einsum(
                "lk,gkm->glm",
                upper_mask,
                infrared_radiance * damped[:, :strata_mesh] * jnp.expm1(-thickness),
                precision=lax.Precision.HIGHEST,
            )
        )
        sunbeam = (
            solar_part[:, None, None]
            * illuminated_marker[None, None, :]
            * jnp.exp(-column_depth / overhead_angle_value[None, None, :])
        )
        fluxes = downward - upward + sunbeam
        return jnp.sum(fluxes[:, :strata_mesh] - fluxes[:, 1:], axis=0)

    spectral = lax.map(
        layer_pass,
        (
            arid_multiplier.reshape(bundles, bundle, strata_mesh),
            moisture_multiplier.reshape(bundles, bundle),
            radiance_share_table.reshape(bundles, bundle),
            sunshine_multiplier.reshape(bundles, bundle),
            profile_window.reshape(bundles, bundle, profile_window.shape[1]),
        ),
    )
    return jnp.sum(spectral, axis=0)


def advance(atmosphere_variables, spreading_number):
    padded = with_halo(atmosphere_variables, (("tile", 2),), 1)
    eastern = jnp.roll(atmosphere_variables, -1, axis=3)
    western = jnp.roll(atmosphere_variables, 1, axis=3)
    return atmosphere_variables + spreading_number * (
        padded[:, :, :-2] + padded[:, :, 2:] + eastern + western - 4.0 * atmosphere_variables
    )


def on_device(
    kelvin_profile,
    moisture_profile,
    spreading_number,
    overhead_angle_measure,
    illuminated_mask,
    radiating_tiles,
    cloudy_member_factors,
    arid_opacity_table,
    moisture_attenuation,
    blackbody_share,
    insolation_per_quadrature,
):
    strata_mesh, parallel_band_sequence, meridian_boxes = kelvin_profile.shape
    atmosphere_variables = jnp.stack([kelvin_profile, moisture_profile])
    for repeat in range(2):
        atmosphere_variables = advance(atmosphere_variables, spreading_number)
    temp_dyn = atmosphere_variables[0]
    vapour_next = atmosphere_variables[1]
    columns = parallel_band_sequence * meridian_boxes
    tile_count = lax.axis_size("tile")
    capacity = cloudy_member_factors.shape[1] // tile_count
    slots = tile_count * capacity
    owner_ids = radiating_tiles[:, 0]
    matches = (owner_ids[:, None] == jnp.arange(tile_count, dtype=jnp.int32)[None, :]).astype(
        jnp.int32
    )
    position = jnp.sum((jnp.cumsum(matches, axis=0) - 1) * matches, axis=1)
    slot_index = owner_ids * capacity + position
    overhead_angle_value = overhead_angle_measure.reshape(columns)
    sunlit_local = overhead_angle_value * illuminated_mask.reshape(columns).astype(jnp.float32)
    column_rows = jnp.concatenate(
        [temp_dyn.reshape(strata_mesh, columns).T, vapour_next.reshape(strata_mesh, columns).T],
        axis=1,
    )
    outgoing = (
        jnp.zeros((slots, 2 * strata_mesh), jnp.float32)
        .at[slot_index]
        .set(column_rows)
        .reshape(tile_count, capacity, 2 * strata_mesh)
    )
    sun_rows = jnp.stack([overhead_angle_value, sunlit_local], axis=1)
    blank = jnp.stack([jnp.ones((slots,), jnp.float32), jnp.zeros((slots,), jnp.float32)], axis=1)
    sun_out = blank.at[slot_index].set(sun_rows).reshape(tile_count, capacity, 2)
    incoming, sun_in = (
        lax.all_to_all(outgoing, "tile", split_axis=0, concat_axis=0, tiled=True),
        lax.all_to_all(sun_out, "tile", split_axis=0, concat_axis=0, tiled=True),
    )
    incoming = incoming.reshape(slots, 2 * strata_mesh)
    sun_in = sun_in.reshape(slots, 2)
    partial_value = evaluate_warming(
        incoming[:, :strata_mesh].T,
        incoming[:, strata_mesh:].T,
        sun_in[:, 0],
        sun_in[:, 1],
        cloudy_member_factors,
        arid_opacity_table,
        moisture_attenuation,
        blackbody_share,
        insolation_per_quadrature,
    )
    summed = lax.psum(partial_value, "grp")
    returning = lax.all_to_all(
        summed.T.reshape(tile_count, capacity, strata_mesh),
        "tile",
        split_axis=0,
        concat_axis=0,
        tiled=True,
    )
    total_heat = returning.reshape(slots, strata_mesh)[slot_index].T
    heating = (total_heat / NG).reshape(strata_mesh, parallel_band_sequence, meridian_boxes)
    return (heating, temp_dyn + heating, vapour_next)


def solution(mesh):
    in_specs = (
        P(None, "tile", None),
        P(None, "tile", None),
        P("tile", None),
        P("tile", None),
        P("tile", None),
        P("tile", None),
        P("grp", "tile"),
        P("grp", None),
        P("grp"),
        P("grp"),
        P("grp"),
    )
    out_specs = (P(None, "tile", None), P(None, "tile", None), P(None, "tile", None))
    return jax.shard_map(
        on_device, mesh=mesh, in_specs=in_specs, out_specs=out_specs, check_vma=False
    )
```

profile of v0, /device:TPU:1, one launch (start us, length us, event | category | flops | bytes accessed | tf_op | source)
XLA Modules:
  0.0 282.9 jit_solution(3957127956137913107)
XLA Ops:
  7.2 1.0 copy.57
  8.2 1.0 copy.58
  9.2 8.8 %collective-permute-start.1 = (f32[2,90,1,256]{1,3,2,0:T(8,128)S(1)}, f32[2,90,1,256]{1,3,2,0:T(8,128)S(1)}, u32[]{:S(2)}, u32[]{:S(2)}) collective-permute-start(f32[2,90,1,256]{1,3,2,0:T(8,128)S(1)} %pad_maximum_fusion), channel_id=1, source_target_pairs={{4,0},{8,4},{12,8},{16,12},{20,16},{24,20},{28,24},{32,28},{36,32}... | collective-permute-start | bytes 552968 | tf_op jit(solution)/shard_map/ppermute | solution.py:18
  18.0 1.9 collective-permute-start
  24.2 1.3 scatter_fusion
  25.5 1.5 copy.61
  27.0 12.7 %all-to-all-start.1 = ((f32[128,4,2]{1,2,0:T(2,128)}), f32[128,4,2]{1,2,0:T(2,128)S(1)}, u32[]{:S(2)}, u32[]{:S(2)}) async-start(f32[128,4,2]{1,2,0:T(2,128)} %copy.61), calls=%async_computation.1 | async-start | bytes 262144 | tf_op jit(solution)/shard_map/all_to_all | solution.py:146
  39.9 2.8 collective-permute-start.3
  42.7 2.8 collective-permute-start.2
  45.5 2.3 collective-permute-done.3
  48.9 1.7 scatter_custom_fusion
  50.6 0.9 reshape.191
  52.4 15.6 %all-to-all-start = ((f32[128,4,180]{2,1,0:T(4,128)}), f32[128,4,180]{2,1,0:T(4,128)}, u32[]{:S(2)}, u32[]{:S(2)}) async-start(f32[128,4,180]{2,1,0:T(4,128)} %reshape.191), calls=%async_computation | async-start | bytes 1048576 | tf_op jit(solution)/shard_map/all_to_all | solution.py:145
  68.3 1.3 reshape.193
  69.7 1.3 reshape.194
  71.0 1.6 reshape.189
  74.2 14.0 %all-to-all-done = f32[128,4,180]{2,1,0:T(4,128)} async-done(((f32[128,4,180]{2,1,0:T(4,128)}), f32[128,4,180]{2,1,0:T(4,128)}, u32[]{:S(2)}, u32[]{:S(2)}) %all-to-all-start) | async-done | bytes 368672 | tf_op jit(solution)/shard_map/all_to_all | solution.py:145
  88.2 2.0 reshape.192
  90.2 2.0 slice_bitcast_fusion
  92.2 1.1 copy.64
  93.3 1.1 copy.63
  94.4 103.7 %while.12 = (s32[]{:T(128)}, f32[14,90,512]{2,1,0:T(8,128)S(1)}, f32[14,4,90]{2,1,0:T(4,128)}, f32[14,4]{1,0:T(8,128)S(1)}, f32[14,4,512]{2,1,0:T(4,128)}, /*ind...) while((s32[]{:T(128)}, f32[14,90,512]{2,1,0:T(8,128)S(1)}, ...), condition=%wide.region_7.8_spmd.clone.clone, body=%wide.region_5.7_spmd.clone.clone.sunk | while | flops 608476160 | bytes 12221821 | solution.py:78
  97.3 0.9 fusion.78
  98.7 1.4 fusion.79
  100.2 1.5 fusion.81
  104.7 0.9 fusion.78
  106.1 1.4 fusion.79
  107.6 1.5 fusion.81
  112.2 0.9 fusion.78
  113.5 1.4 fusion.79
  115.0 1.5 fusion.81
  119.6 0.9 fusion.78
  121.0 1.4 fusion.79
  122.4 1.5 fusion.81
  127.0 0.9 fusion.78
  128.3 1.4 fusion.79
  129.8 1.5 fusion.81
  134.4 0.9 fusion.78
  135.8 1.4 fusion.79
  137.2 1.5 fusion.81
  141.8 0.9 fusion.78
  143.2 1.4 fusion.79
  144.6 1.5 fusion.81
  149.2 0.9 fusion.78
  150.6 1.4 fusion.79
  152.0 1.5 fusion.81
  156.6 0.9 fusion.78
  158.0 1.4 fusion.79
  159.4 1.5 fusion.81
  164.0 0.9 fusion.78
  165.4 1.4 fusion.79
  166.8 1.5 fusion.81
  171.4 0.9 fusion.78
  172.8 1.4 fusion.79
  174.2 1.5 fusion.81
  180.2 1.4 fusion.79
  181.6 1.5 fusion.81
  187.6 1.4 fusion.79
  189.0 1.5 fusion.81
  195.0 1.4 fusion.79
  196.4 1.5 fusion.81
  199.2 42.9 %all-reduce.2.cloned.1.call-done = f32[128,4,90]{2,1,0:T(4,128)} async-done(((f32[128,4,90]{2,1,0:T(4,128)}), f32[128,4,90]{2,1,0:T(4,128)}) %all-reduce.2.cloned.1.call-update) | async-done | bytes 184336 | tf_op jit(solution)/shard_map/psum | solution.py:161
  242.1 16.4 %all-to-all-start.2 = ((f32[128,4,90]{2,1,0:T(4,128)}), f32[128,4,90]{2,1,0:T(4,128)S(1)}, u32[]{:S(2)}, u32[]{:S(2)}) async-start(f32[128,4,90]{2,1,0:T(4,128)} %all-reduce.2.cloned.1.call-done), calls=%async_computation.2 | async-start | bytes 524288 | tf_op jit(solution)/shard_map/all_to_all | solution.py:162
  259.3 14.5 %all-to-all-done.2 = f32[128,4,90]{2,1,0:T(4,128)S(1)} async-done(((f32[128,4,90]{2,1,0:T(4,128)}), f32[128,4,90]{2,1,0:T(4,128)S(1)}, u32[]{:S(2)}, u32[]{:S(2)}) %all-to-all-start.2) | async-done | bytes 184352 | tf_op jit(solution)/shard_map/all_to_all | solution.py:162
  (233 shorter events, 63.3 us)
Async XLA Ops:
  7.2 17.0 %copy-start = (f32[512,2]{1,0:T(8,128)S(1)}, f32[512,2]{1,0:T(8,128)}, u32[]{:S(2)}) copy-start(f32[512,2]{1,0:T(8,128)} %constant.42.clone.1) | copy-start | bytes 12292
  9.2 30.5 %collective-permute-start.1 = (f32[2,90,1,256]{1,3,2,0:T(8,128)S(1)}, f32[2,90,1,256]{1,3,2,0:T(8,128)S(1)}, u32[]{:S(2)}, u32[]{:S(2)}) collective-permute-start(f32[2,90,1,256]{1,3,2,0:T(8,128)S(1)} %pad_maximum_fusion), channel_id=1, source_target_pairs={{4,0},{8,4},{12,8},{16,12},{20,16},{24,20},{28,24},{32,28},{36,32}... | collective-permute-start | bytes 552968 | tf_op jit(solution)/shard_map/ppermute | solution.py:18
  18.0 21.7 %collective-permute-start = (f32[2,90,1,256]{1,3,2,0:T(8,128)S(1)}, f32[2,90,1,256]{1,3,2,0:T(8,128)S(1)}, u32[]{:S(2)}, u32[]{:S(2)}) collective-permute-start(f32[2,90,1,256]{1,3,2,0:T(8,128)S(1)} %pad_maximum_fusion), channel_id=1, source_target_pairs={{0,4},{4,8},{8,12},{12,16},{16,20},{20,24},{24,28},{28,32},{32,36}... | collective-permute-start | bytes 552968 | tf_op jit(solution)/shard_map/ppermute | solution.py:15
  20.7 19.0 %copy-start.2 = (f32[1,256]{1,0:T(1,128)S(1)}, f32[1,256]{1,0:T(1,128)}, u32[]{:S(2)}) copy-start(f32[1,256]{1,0:T(1,128)} %param.15) | copy-start | bytes 3076
  27.0 25.5 %all-to-all-start.1 = ((f32[128,4,2]{1,2,0:T(2,128)}), f32[128,4,2]{1,2,0:T(2,128)S(1)}, u32[]{:S(2)}, u32[]{:S(2)}) async-start(f32[128,4,2]{1,2,0:T(2,128)} %copy.61), calls=%async_computation.1 | async-start | bytes 262144 | tf_op jit(solution)/shard_map/all_to_all | solution.py:146
  39.9 8.0 %collective-permute-start.3 = (f32[2,90,1,256]{1,3,2,0:T(8,128)S(1)}, f32[2,90,1,256]{1,3,2,0:T(8,128)S(1)}, u32[]{:S(2)}, u32[]{:S(2)}) collective-permute-start(f32[2,90,1,256]{1,3,2,0:T(8,128)S(1)} %fusion.45), channel_id=1, source_target_pairs={{4,0},{8,4},{12,8},{16,12},{20,16},{24,20},{28,24},{32,28},{36,32}... | collective-permute-start | bytes 552968 | tf_op jit(solution)/shard_map/ppermute | solution.py:18
  42.7 6.1 %collective-permute-start.2 = (f32[2,90,1,256]{1,3,2,0:T(8,128)S(1)}, f32[2,90,1,256]{1,3,2,0:T(8,128)S(1)}, u32[]{:S(2)}, u32[]{:S(2)}) collective-permute-start(f32[2,90,1,256]{1,3,2,0:T(8,128)S(1)} %fusion.45), channel_id=1, source_target_pairs={{0,4},{4,8},{8,12},{12,16},{16,20},{20,24},{24,28},{28,32},{32,36}... | collective-permute-start | bytes 552968 | tf_op jit(solution)/shard_map/ppermute | solution.py:15
  45.5 22.7 %copy-start.4 = (f32[56]{0:T(128)S(1)}, f32[56]{0:T(128)}, u32[]{:S(2)}) copy-start(f32[56]{0:T(128)} %param.21) | copy-start | bytes 676
  52.4 15.6 %copy-start.1 = (f32[128,4,2]{1,2,0:T(2,128)}, f32[128,4,2]{1,2,0:T(2,128)S(1)}, u32[]{:S(2)}) copy-start(f32[128,4,2]{1,2,0:T(2,128)S(1)} %all-to-all-done.1) | copy-start | bytes 12292
  52.4 35.8 %all-to-all-start = ((f32[128,4,180]{2,1,0:T(4,128)}), f32[128,4,180]{2,1,0:T(4,128)}, u32[]{:S(2)}, u32[]{:S(2)}) async-start(f32[128,4,180]{2,1,0:T(4,128)} %reshape.191), calls=%async_computation | async-start | bytes 1048576 | tf_op jit(solution)/shard_map/all_to_all | solution.py:145
  68.0 174.1 %all-reduce.2.cloned.1.call-start = ((), (), s32[]{:S(2)}) async-start(), calls=%async_computation.3 | async-start | bytes 524288 | tf_op jit(solution)/shard_map/psum | solution.py:161
  98.4 1.7 copy-start.3
  105.9 1.7 copy-start.3
  113.3 1.7 copy-start.3
  120.7 1.7 copy-start.3
  128.1 1.7 copy-start.3
  135.5 1.7 copy-start.3
  142.9 1.7 copy-start.3
  150.3 1.7 copy-start.3
  157.7 1.7 copy-start.3
  165.1 1.7 copy-start.3
  172.5 1.7 copy-start.3
  179.9 1.7 copy-start.3
  187.3 1.7 copy-start.3
  194.7 1.7 copy-start.3
  242.1 31.7 %all-to-all-start.2 = ((f32[128,4,90]{2,1,0:T(4,128)}), f32[128,4,90]{2,1,0:T(4,128)S(1)}, u32[]{:S(2)}, u32[]{:S(2)}) async-start(f32[128,4,90]{2,1,0:T(4,128)} %all-reduce.2.cloned.1.call-done), calls=%async_computation.2 | async-start | bytes 524288 | tf_op jit(solution)/shard_map/all_to_all | solution.py:162
Sparse Core Ops, SparseCore 0:
  199.4 42.6 all-reduce.1
where the time goes:
time: 286 us; the launch traced here: 283 us
  waiting for transfers between devices  75.5 us (26%)
  starting transfers between devices  61.2 us (21%)
  matrix products  54.1 us (19%)
  local copies, waits for them, and re-layouts  52.1 us (18%)
  other arithmetic  24.2 us (8%)
  between operations  14.3 us (5%)
    psum x1, waiting for transfers between devices, on_device(): summed = lax.psum(partial_value, 'grp')  42.9 us
    dot_general x14, matrix products, layer_pass(): jnp.einsum('lk,gkm->glm', lower_mask, infrared_radiance * growth[:, :stra...  21.2 us
    dot_general x14, matrix products, layer_pass(): jnp.einsum('lk,gkm->glm', upper_mask, infrared_radiance * damped[:, :stra...  19.8 us
    all_to_all x1, starting transfers between devices, on_device(): lax.all_to_all(summed.T.reshape(tile_count, capacity, strata_mesh), 'tile...  16.4 us
    all_to_all x1, starting transfers between devices, on_device(): lax.all_to_all(outgoing, 'tile', split_axis=0, concat_axis=0, tiled=True)  15.6 us
    all_to_all x1, waiting for transfers between devices, on_device(): lax.all_to_all(summed.T.reshape(tile_count, capacity, strata_mesh), 'tile...  14.5 us
    all_to_all x1, waiting for transfers between devices, on_device(): lax.all_to_all(outgoing, 'tile', split_axis=0, concat_axis=0, tiled=True)  14 us
    dot_general x14, matrix products, layer_pass(): jnp.einsum('lk,gkm->glm', lower_mask, thickness, precision=lax.Precision....  13.1 us
  transfers between devices with their start and end apart: 8, of which 6 were waited for; matrix products, arithmetic and copies ran while one was open for 6% of the time, Pallas kernels for 0%

commit v1 on v0

--- a/solution.py
+++ b/solution.py
@@ -158,7 +158,9 @@
         blackbody_share,
         insolation_per_quadrature,
     )
-    summed = lax.psum(partial_value, "grp")
+    summed = partial_value
+    for hop in (1, 2):
+        summed = summed + lax.ppermute(summed, "grp", [(dev, dev ^ hop) for dev in range(4)])
     returning = lax.all_to_all(
         summed.T.reshape(tile_count, capacity, strata_mesh),
         "tile",

time: 286 us -> 238 us (0.83)
  waiting for transfers between devices: 75.5 us -> 43.3 us
  between operations: 14.3 us -> 0.95 us
    psum x1 -> x0, waiting for transfers between devices: 42.9 us -> none  [on_device(): summed = lax.psum(partial_value, 'grp')]
    ppermute x0 -> x2, waiting for transfers between devices: none -> 10.4 us  [on_device(): lax.ppermute(summed, 'grp', [(dev, dev ^ hop) for dev in range(4)])]
    all_to_all x1, starting transfers between devices: 16.4 us -> 6.45 us  [on_device(): lax.all_to_all(summed.T.reshape(tile_count, capacity, strata_mesh), 'tile...]
    ppermute x0 -> x2, starting transfers between devices: none -> 7.76 us  [on_device(): lax.ppermute(summed, 'grp', [(dev, dev ^ hop) for dev in range(4)])]
  transfers between devices with their start and end apart: 8 -> 9, of which waited for: 6 -> 7; matrix products, arithmetic and copies ran while one was open for 6% -> 7% of each run, Pallas kernels for 0% -> 0%
where the time goes in v1:
time: 238 us; the launch traced here: 236 us
  starting transfers between devices  58.9 us (25%)
  matrix products  54.1 us (23%)
  local copies, waits for them, and re-layouts  52.8 us (22%)
  waiting for transfers between devices  43.3 us (18%)
  other arithmetic  24.3 us (10%)
    dot_general x14, matrix products, layer_pass(): jnp.einsum('lk,gkm->glm', lower_mask, infrared_radiance * growth[:, :stra...  21.2 us
    dot_general x14, matrix products, layer_pass(): jnp.einsum('lk,gkm->glm', upper_mask, infrared_radiance * damped[:, :stra...  19.8 us
    all_to_all x1, starting transfers between devices, on_device(): lax.all_to_all(outgoing, 'tile', split_axis=0, concat_axis=0, tiled=True)  15.7 us
    all_to_all x1, waiting for transfers between devices, on_device(): lax.all_to_all(summed.T.reshape(tile_count, capacity, strata_mesh), 'tile...  14.6 us
    all_to_all x1, waiting for transfers between devices, on_device(): lax.all_to_all(outgoing, 'tile', split_axis=0, concat_axis=0, tiled=True)  14.2 us
    dot_general x14, matrix products, layer_pass(): jnp.einsum('lk,gkm->glm', lower_mask, thickness, precision=lax.Precision....  13.1 us
    all_to_all x1, starting transfers between devices, on_device(): lax.all_to_all(sun_out, 'tile', split_axis=0, concat_axis=0, tiled=True)  12.7 us
    ppermute x2, starting transfers between devices, with_halo(): lax.ppermute(lax.slice_in_dim(block, 0, width, axis=dim), axis, backward)  11.6 us
  transfers between devices with their start and end apart: 9, of which 7 were waited for; matrix products, arithmetic and copies ran while one was open for 7% of the time, Pallas kernels for 0%

profile of v1, /device:TPU:1, one launch (start us, length us, event | category | flops | bytes accessed | tf_op | source)
XLA Modules:
  0.0 235.7 jit_solution(16176982722219651788)
XLA Ops:
  0.6 1.0 copy.57
  1.7 1.0 copy.58
  2.7 8.8 %collective-permute-start.1 = (f32[2,90,1,256]{1,3,2,0:T(8,128)S(1)}, f32[2,90,1,256]{1,3,2,0:T(8,128)S(1)}, u32[]{:S(2)}, u32[]{:S(2)}) collective-permute-start(f32[2,90,1,256]{1,3,2,0:T(8,128)S(1)} %pad_maximum_fusion), channel_id=1, source_target_pairs={{4,0},{8,4},{12,8},{16,12},{20,16},{24,20},{28,24},{32,28},{36,32}... | collective-permute-start | bytes 552968 | tf_op jit(solution)/shard_map/ppermute | solution.py:18
  11.5 1.9 collective-permute-start
  17.6 1.3 scatter_fusion
  18.9 1.5 copy.61
  20.4 12.7 %all-to-all-start.1 = ((f32[128,4,2]{1,2,0:T(2,128)}), f32[128,4,2]{1,2,0:T(2,128)S(1)}, u32[]{:S(2)}, u32[]{:S(2)}) async-start(f32[128,4,2]{1,2,0:T(2,128)} %copy.61), calls=%async_computation.1 | async-start | bytes 262144 | tf_op jit(solution)/shard_map/all_to_all | solution.py:146
  33.4 2.8 %collective-permute-start.3 = (f32[2,90,1,256]{1,3,2,0:T(8,128)S(1)}, f32[2,90,1,256]{1,3,2,0:T(8,128)S(1)}, u32[]{:S(2)}, u32[]{:S(2)}) collective-permute-start(f32[2,90,1,256]{1,3,2,0:T(8,128)S(1)} %fusion.45), channel_id=1, source_target_pairs={{4,0},{8,4},{12,8},{16,12},{20,16},{24,20},{28,24},{32,28},{36,32}... | collective-permute-start | bytes 552968 | tf_op jit(solution)/shard_map/ppermute | solution.py:18
  36.2 2.8 %collective-permute-start.2 = (f32[2,90,1,256]{1,3,2,0:T(8,128)S(1)}, f32[2,90,1,256]{1,3,2,0:T(8,128)S(1)}, u32[]{:S(2)}, u32[]{:S(2)}) collective-permute-start(f32[2,90,1,256]{1,3,2,0:T(8,128)S(1)} %fusion.45), channel_id=1, source_target_pairs={{0,4},{4,8},{8,12},{12,16},{16,20},{20,24},{24,28},{28,32},{32,36}... | collective-permute-start | bytes 552968 | tf_op jit(solution)/shard_map/ppermute | solution.py:15
  39.0 2.3 collective-permute-done.3
  42.4 1.7 scatter_custom_fusion
  44.1 1.0 reshape.191
  46.5 15.7 %all-to-all-start = ((f32[128,4,180]{2,1,0:T(4,128)}), f32[128,4,180]{2,1,0:T(4,128)}, u32[]{:S(2)}, u32[]{:S(2)}) async-start(f32[128,4,180]{2,1,0:T(4,128)} %reshape.191), calls=%async_computation | async-start | bytes 1048576 | tf_op jit(solution)/shard_map/all_to_all | solution.py:145
  62.3 1.3 reshape.193
  63.6 1.3 reshape.194
  65.0 1.6 reshape.189
  68.2 14.2 %all-to-all-done = f32[128,4,180]{2,1,0:T(4,128)} async-done(((f32[128,4,180]{2,1,0:T(4,128)}), f32[128,4,180]{2,1,0:T(4,128)}, u32[]{:S(2)}, u32[]{:S(2)}) %all-to-all-start) | async-done | bytes 368672 | tf_op jit(solution)/shard_map/all_to_all | solution.py:145
  82.4 2.0 reshape.192
  84.4 2.0 slice_bitcast_fusion
  86.4 1.1 copy.64
  87.5 1.1 copy.63
  88.6 103.7 %while.12 = (s32[]{:T(128)}, f32[14,90,512]{2,1,0:T(8,128)S(1)}, f32[14,4,90]{2,1,0:T(4,128)}, f32[14,4]{1,0:T(8,128)S(1)}, f32[14,4,512]{2,1,0:T(4,128)}, /*ind...) while((s32[]{:T(128)}, f32[14,90,512]{2,1,0:T(8,128)S(1)}, ...), condition=%wide.region_7.8_spmd.clone.clone, body=%wide.region_5.7_spmd.clone.clone.sunk | while | flops 608476160 | bytes 12221821 | solution.py:78
  91.5 0.9 fusion.78
  92.9 1.4 fusion.79
  94.3 1.5 fusion.81
  98.9 0.9 fusion.78
  100.3 1.4 fusion.79
  101.7 1.5 fusion.81
  106.3 0.9 fusion.78
  107.7 1.4 fusion.79
  109.1 1.5 fusion.81
  113.7 0.9 fusion.78
  115.1 1.4 fusion.79
  116.5 1.5 fusion.81
  121.1 0.9 fusion.78
  122.5 1.4 fusion.79
  123.9 1.5 fusion.81
  128.5 0.9 fusion.78
  129.9 1.4 fusion.79
  131.3 1.5 fusion.81
  135.9 0.9 fusion.78
  137.3 1.4 fusion.79
  138.7 1.5 fusion.81
  143.3 0.9 fusion.78
  144.7 1.4 fusion.79
  146.2 1.5 fusion.81
  152.1 1.4 fusion.79
  153.6 1.5 fusion.81
  159.5 1.4 fusion.79
  161.0 1.5 fusion.81
  166.9 1.4 fusion.79
  168.4 1.5 fusion.81
  174.3 1.4 fusion.79
  175.8 1.5 fusion.81
  181.7 1.4 fusion.79
  183.2 1.5 fusion.81
  189.1 1.4 fusion.79
  190.6 1.5 fusion.81
  192.5 3.1 %collective-permute-start.4 = (f32[90,512]{1,0:T(8,128)S(1)}, f32[90,512]{1,0:T(8,128)S(1)}, u32[]{:S(2)}, u32[]{:S(2)}) collective-permute-start(f32[90,512]{1,0:T(8,128)S(1)} %reduce_sum.31), channel_id=1, source_target_pairs={{0,1},{1,0},{2,3},{3,2},{4,5},{5,4},{6,7},{7,6},{8,9},{9,8},{10,11... | collective-permute-start | bytes 552968 | tf_op jit(solution)/shard_map/ppermute | solution.py:163
  195.7 5.6 %collective-permute-done.4 = f32[90,512]{1,0:T(8,128)S(1)} collective-permute-done((f32[90,512]{1,0:T(8,128)S(1)}, f32[90,512]{1,0:T(8,128)S(1)}, u32[]{:S(2)}, u32[]{:S(2)}) %collective-permute-start.4) | collective-permute-done | bytes 184352 | tf_op jit(solution)/shard_map/ppermute | solution.py:163
  201.3 4.6 %collective-permute-start.5 = (f32[90,512]{1,0:T(8,128)S(1)}, f32[90,512]{1,0:T(8,128)S(1)}, u32[]{:S(2)}, u32[]{:S(2)}) collective-permute-start(f32[90,512]{1,0:T(8,128)S(1)} %add.75), channel_id=1, source_target_pairs={{0,2},{1,3},{2,0},{3,1},{4,6},{5,7},{6,4},{7,5},{8,10},{9,11},{10,... | collective-permute-start | bytes 552968 | tf_op jit(solution)/shard_map/ppermute | solution.py:163
  206.0 4.8 %collective-permute-done.5 = f32[90,512]{1,0:T(8,128)S(1)} collective-permute-done((f32[90,512]{1,0:T(8,128)S(1)}, f32[90,512]{1,0:T(8,128)S(1)}, u32[]{:S(2)}, u32[]{:S(2)}) %collective-permute-start.5) | collective-permute-done | bytes 184352 | tf_op jit(solution)/shard_map/ppermute | solution.py:163
  211.6 6.5 %all-to-all-start.2 = ((f32[128,4,90]{2,1,0:T(4,128)}), f32[128,4,90]{2,1,0:T(4,128)S(1)}, u32[]{:S(2)}, u32[]{:S(2)}) async-start(f32[128,4,90]{2,1,0:T(4,128)} %bitcast.21), calls=%async_computation.2 | async-start | bytes 524288 | tf_op jit(solution)/shard_map/all_to_all | solution.py:164
  218.8 14.6 %all-to-all-done.2 = f32[128,4,90]{2,1,0:T(4,128)S(1)} async-done(((f32[128,4,90]{2,1,0:T(4,128)}), f32[128,4,90]{2,1,0:T(4,128)S(1)}, u32[]{:S(2)}, u32[]{:S(2)}) %all-to-all-start.2) | async-done | bytes 184352 | tf_op jit(solution)/shard_map/all_to_all | solution.py:164
  (236 shorter events, 66.5 us)
Async XLA Ops:
  0.6 17.0 %copy-start = (f32[512,2]{1,0:T(8,128)S(1)}, f32[512,2]{1,0:T(8,128)}, u32[]{:S(2)}) copy-start(f32[512,2]{1,0:T(8,128)} %constant.42.clone.1) | copy-start | bytes 12292
  2.7 30.5 %collective-permute-start.1 = (f32[2,90,1,256]{1,3,2,0:T(8,128)S(1)}, f32[2,90,1,256]{1,3,2,0:T(8,128)S(1)}, u32[]{:S(2)}, u32[]{:S(2)}) collective-permute-start(f32[2,90,1,256]{1,3,2,0:T(8,128)S(1)} %pad_maximum_fusion), channel_id=1, source_target_pairs={{4,0},{8,4},{12,8},{16,12},{20,16},{24,20},{28,24},{32,28},{36,32}... | collective-permute-start | bytes 552968 | tf_op jit(solution)/shard_map/ppermute | solution.py:18
  11.5 21.7 %collective-permute-start = (f32[2,90,1,256]{1,3,2,0:T(8,128)S(1)}, f32[2,90,1,256]{1,3,2,0:T(8,128)S(1)}, u32[]{:S(2)}, u32[]{:S(2)}) collective-permute-start(f32[2,90,1,256]{1,3,2,0:T(8,128)S(1)} %pad_maximum_fusion), channel_id=1, source_target_pairs={{0,4},{4,8},{8,12},{12,16},{16,20},{20,24},{24,28},{28,32},{32,36}... | collective-permute-start | bytes 552968 | tf_op jit(solution)/shard_map/ppermute | solution.py:15
  14.2 19.0 %copy-start.2 = (f32[1,256]{1,0:T(1,128)S(1)}, f32[1,256]{1,0:T(1,128)}, u32[]{:S(2)}) copy-start(f32[1,256]{1,0:T(1,128)} %param.15) | copy-start | bytes 3076
  20.4 25.4 %all-to-all-start.1 = ((f32[128,4,2]{1,2,0:T(2,128)}), f32[128,4,2]{1,2,0:T(2,128)S(1)}, u32[]{:S(2)}, u32[]{:S(2)}) async-start(f32[128,4,2]{1,2,0:T(2,128)} %copy.61), calls=%async_computation.1 | async-start | bytes 262144 | tf_op jit(solution)/shard_map/all_to_all | solution.py:146
  33.4 8.0 %collective-permute-start.3 = (f32[2,90,1,256]{1,3,2,0:T(8,128)S(1)}, f32[2,90,1,256]{1,3,2,0:T(8,128)S(1)}, u32[]{:S(2)}, u32[]{:S(2)}) collective-permute-start(f32[2,90,1,256]{1,3,2,0:T(8,128)S(1)} %fusion.45), channel_id=1, source_target_pairs={{4,0},{8,4},{12,8},{16,12},{20,16},{24,20},{28,24},{32,28},{36,32}... | collective-permute-start | bytes 552968 | tf_op jit(solution)/shard_map/ppermute | solution.py:18
  36.2 6.1 %collective-permute-start.2 = (f32[2,90,1,256]{1,3,2,0:T(8,128)S(1)}, f32[2,90,1,256]{1,3,2,0:T(8,128)S(1)}, u32[]{:S(2)}, u32[]{:S(2)}) collective-permute-start(f32[2,90,1,256]{1,3,2,0:T(8,128)S(1)} %fusion.45), channel_id=1, source_target_pairs={{0,4},{4,8},{8,12},{12,16},{16,20},{20,24},{24,28},{28,32},{32,36}... | collective-permute-start | bytes 552968 | tf_op jit(solution)/shard_map/ppermute | solution.py:15
  39.0 23.2 %copy-start.4 = (f32[56]{0:T(128)S(1)}, f32[56]{0:T(128)}, u32[]{:S(2)}) copy-start(f32[56]{0:T(128)} %param.21) | copy-start | bytes 676
  45.8 0.7 copy-start.1
  46.5 35.9 %all-to-all-start = ((f32[128,4,180]{2,1,0:T(4,128)}), f32[128,4,180]{2,1,0:T(4,128)}, u32[]{:S(2)}, u32[]{:S(2)}) async-start(f32[128,4,180]{2,1,0:T(4,128)} %reshape.191), calls=%async_computation | async-start | bytes 1048576 | tf_op jit(solution)/shard_map/all_to_all | solution.py:145
  92.6 1.7 copy-start.3
  100.0 1.7 copy-start.3
  107.4 1.7 copy-start.3
  114.8 1.7 copy-start.3
  122.2 1.7 copy-start.3
  129.6 1.7 copy-start.3
  137.0 1.7 copy-start.3
  144.4 1.7 copy-start.3
  151.8 1.7 copy-start.3
  159.2 1.7 copy-start.3
  166.6 1.7 copy-start.3
  174.1 1.7 copy-start.3
  181.5 1.7 copy-start.3
  188.9 1.7 copy-start.3
  192.5 8.8 %collective-permute-start.4 = (f32[90,512]{1,0:T(8,128)S(1)}, f32[90,512]{1,0:T(8,128)S(1)}, u32[]{:S(2)}, u32[]{:S(2)}) collective-permute-start(f32[90,512]{1,0:T(8,128)S(1)} %reduce_sum.31), channel_id=1, source_target_pairs={{0,1},{1,0},{2,3},{3,2},{4,5},{5,4},{6,7},{7,6},{8,9},{9,8},{10,11... | collective-permute-start | bytes 552968 | tf_op jit(solution)/shard_map/ppermute | solution.py:163
  201.3 9.4 %collective-permute-start.5 = (f32[90,512]{1,0:T(8,128)S(1)}, f32[90,512]{1,0:T(8,128)S(1)}, u32[]{:S(2)}, u32[]{:S(2)}) collective-permute-start(f32[90,512]{1,0:T(8,128)S(1)} %add.75), channel_id=1, source_target_pairs={{0,2},{1,3},{2,0},{3,1},{4,6},{5,7},{6,4},{7,5},{8,10},{9,11},{10,... | collective-permute-start | bytes 552968 | tf_op jit(solution)/shard_map/ppermute | solution.py:163
  211.6 21.8 %all-to-all-start.2 = ((f32[128,4,90]{2,1,0:T(4,128)}), f32[128,4,90]{2,1,0:T(4,128)S(1)}, u32[]{:S(2)}, u32[]{:S(2)}) async-start(f32[128,4,90]{2,1,0:T(4,128)} %bitcast.21), calls=%async_computation.2 | async-start | bytes 524288 | tf_op jit(solution)/shard_map/all_to_all | solution.py:164
